TPU v7x, 512 devices: a whole 4x8x8 slice. The times are simulated.
512 devices in a mesh: gx: 32 (over y, x), gy: 16 (over z, core).
Axes of the slice: x: 4, y: 8, z: 8, core: 2. Of those that a mesh axis runs over, the one named last changes fastest.
Arguments:
- panel: bfloat16 [32, 16, 2, 128, 1024], P('gx', 'gy'), may hold values from -0.5 to 0.5
- corner_panel: bfloat16 [32, 16, 2, 24, 128], P('gx', 'gy'), may hold values from -0.5 to 0.5
- interface_diag: float32 [32, 16, 2, 1024], P('gx', 'gy'), may hold values from 0.5 to 2
- coarse_diag: float32 [32, 512], P('gx'), may hold values from 0.5 to 2
- scaling: float32 [32, 16, 8, 128], P('gx', 'gy'), may hold values from 0.5 to 2
- dual_rhs: float32 [32, 16, 8, 128], P('gx', 'gy'), may hold values from -6 to 6
- block_map: int32 [32, 16, 2, 8], P('gx', 'gy'), may hold values from 0 to 39
- corner_map: int32 [32, 16, 2, 24], P('gx', 'gy'), may hold values from 0 to 511
- counts: int32 [32, 16], P('gx', 'gy'), may hold values from 1 to 2, as said below
Outputs:
- multipliers: float32 [32, 16, 8, 128], P('gx', 'gy')
- residual: float32 [32, 16, 8, 128], P('gx', 'gy')
Inputs may be any that keep to these rules, and one draw needn't show every extreme that they name: `counts`: every device holds one or more live subdomains in its first slots; some device has all 2 slots live and some has one.
All inputs are finite; a program needn't handle non-finite values.
Results may differ from a plain program's by a relative error of at most 0.0003.
Values sent between devices are 32-bit elements; how exact they have to be, the bound alone decides.
No kernel may reach another device: no remote copies, remote signals or barrier semaphores. Data moves between devices by JAX's collectives and lax.ppermute only.
A program may use at most 64 MiB of HBM per device.

v0:
```python
import jax
import jax.numpy as jnp
from jax import lax
from jax.sharding import PartitionSpec as P

ITERS = 3


def extended(block, sides, width):
    for axis, dim in sides:
        count = lax.axis_size(axis)
        forward = [(i, i + 1) for i in range(count - 1)]
        backward = [(target, source) for source, target in forward]
        low = lax.ppermute(
            lax.slice_in_dim(block, block.shape[dim] - width, None, axis=dim), axis, forward
        )
        high = lax.ppermute(lax.slice_in_dim(block, 0, width, axis=dim), axis, backward)
        block = jnp.concatenate([low, block, high], axis=dim)
    return block


def weighted_norm(residual, precond):
    return lax.psum(jnp.sum(residual * precond), ("gx", "gy"))


def shards(
    panel,
    corner_panel,
    interface_diag,
    coarse_diag,
    scaling,
    dual_rhs,
    block_map,
    corner_map,
    counts,
):
    highest = lax.Precision.HIGHEST
    slots = panel.shape[2]
    width = panel.shape[4]
    owned = scaling.shape[2]
    block_size = scaling.shape[3]
    blocks_sub = width // block_size
    coarse_size = coarse_diag.shape[1]
    live = (lax.iota(jnp.int32, slots) < counts[0, 0]).astype(jnp.float32)
    factors = panel[0, 0]
    corners = corner_panel[0, 0]
    schur = jnp.einsum("sni,snj->sij", factors, factors, preferred_element_type=jnp.float32)
    width_eye = (lax.iota(jnp.int32, width)[:, None] == lax.iota(jnp.int32, width)[None, :]).astype(
        jnp.float32
    )
    schur = schur + interface_diag[0, 0][:, :, None] * width_eye[None]
    coupling = jnp.einsum("scn,sni->sci", corners, factors, preferred_element_type=jnp.float32)
    corner_block = (
        jnp.einsum("scn,sdn->scd", corners, corners, preferred_element_type=jnp.float32)
        * live[:, None, None]
    )
    local_map = block_map[0, 0]
    signs = jnp.where(local_map < owned, 1.0, -1.0) * live[:, None]
    picker = (local_map[:, :, None] == lax.iota(jnp.int32, 5 * owned)[None, None, :]).astype(
        jnp.float32
    ) * signs[:, :, None]
    coarse_iota = lax.iota(jnp.int32, coarse_size)
    own_hot = (corner_map[0, 0][:, :, None] == coarse_iota[None, None, :]).astype(jnp.float32)
    spread = jnp.einsum("sco,scd->sod", own_hot, corner_block, precision=highest)
    assembled = lax.psum(jnp.einsum("sod,sdp->op", spread, own_hot, precision=highest), "gy")
    coarse_eye = (coarse_iota[:, None] == coarse_iota[None, :]).astype(jnp.float32)
    system = assembled + coarse_diag[0][:, None] * coarse_eye
    lower = jnp.linalg.cholesky(system)

    def operate(field):
        padded = extended(field, (("gx", 0), ("gy", 1)), 1)
        candidates = jnp.concatenate(
            [padded[1, 1], padded[2, 1], padded[0, 1], padded[1, 2], padded[1, 0]], axis=0
        )
        gathered = jnp.einsum("sbk,kc->sbc", picker, candidates, precision=highest).reshape(
            slots, width
        )
        result = jnp.einsum("sij,sj->si", schur, gathered, precision=highest)
        corner_values = (
            jnp.einsum("sci,si->sc", coupling, gathered, precision=highest) * live[:, None]
        )
        coarse_right = lax.psum(
            jnp.einsum("sco,sc->o", own_hot, corner_values, precision=highest), "gy"
        )
        coarse_sol = jax.scipy.linalg.cho_solve((lower, True), coarse_right)
        back_values = jnp.einsum("sco,o->sc", own_hot, coarse_sol, precision=highest)
        result = result + jnp.einsum("sci,sc->si", coupling, back_values, precision=highest)
        contrib = jnp.einsum(
            "sbk,sbc->kc", picker, result.reshape(slots, blocks_sub, block_size), precision=highest
        )
        outgoing = contrib[owned:].reshape(4, owned, block_size)[None, None]
        incoming = extended(outgoing, (("gx", 0), ("gy", 1)), 1)
        image = field[0, 0] + contrib[:owned]
        image = (
            image + incoming[0, 1, 0] + incoming[2, 1, 1] + incoming[1, 0, 2] + incoming[1, 2, 3]
        )
        return image[None, None]

    multipliers = jnp.zeros_like(dual_rhs)
    residual = dual_rhs
    direction = scaling * residual
    norm_now = weighted_norm(residual, direction)
    for sweep_index in range(ITERS):
        image = operate(direction)
        alpha = norm_now / lax.psum(jnp.sum(direction * image), ("gx", "gy"))
        multipliers = multipliers + alpha * direction
        residual = dual_rhs - operate(multipliers)
        precond = scaling * residual
        norm_next = weighted_norm(residual, precond)
        direction = precond + norm_next / norm_now * direction
        norm_now = norm_next
    return (multipliers, residual)


def solution(mesh):
    return jax.shard_map(
        shards,
        mesh=mesh,
        in_specs=(
            P("gx", "gy", None, None, None),
            P("gx", "gy", None, None, None),
            P("gx", "gy", None, None),
            P("gx", None),
            P("gx", "gy", None, None),
            P("gx", "gy", None, None),
            P("gx", "gy", None, None),
            P("gx", "gy", None, None),
            P("gx", "gy"),
        ),
        out_specs=(P("gx", "gy", None, None), P("gx", "gy", None, None)),
        check_vma=False,
    )
```

profile of v0, /device:TPU:225, one launch (start us, length us, event | category | flops | bytes accessed | tf_op | source)
XLA Modules:
  0.0 1205.7 jit_solution(11194242693486896263)
XLA Ops:
  41.8 23.0 %psum.93 = f32[512]{0:T(512)S(1)} all-reduce(f32[512]{0:T(512)S(1)} %bitcast.1267), channel_id=1, replica_groups=mesh['gx'=32,'gy'=16] {'gy'}, use_global_device_ids=true, to_apply=%region_11.12 | all-reduce | flops 512 | bytes 4096 | tf_op jit(solution)/shard_map/psum | solution.py:82
  64.8 9.6 fusion.440
  74.4 64.5 %all-reduce.4.cloned.1.call-done = f32[512,512]{0,1:T(8,128)} async-done(((f32[512,512]{0,1:T(8,128)}), f32[512,512]{0,1:T(8,128)}) %all-reduce.4.cloned.1.call-update) | async-done | bytes 1048592 | tf_op jit(solution)/shard_map/psum | solution.py:65
  142.0 11.7 cholesky.103
  153.9 9.8 custom-call.32
  164.5 11.7 cholesky.215
  176.3 10.2 custom-call.33
  187.6 11.7 cholesky.236
  199.5 9.8 custom-call.34
  210.1 11.9 cholesky.253
  226.6 10.5 while.12
  237.1 40.1 %custom-call.40 = f32[4,128,128]{1,2,0:T(8,128)S(1)} custom-call(f32[4,128,128]{2,1,0:T(8,128)} %get-tuple-element.41), custom_call_target="InvertDiagBlocksLowerTriangular" | custom-call | tf_op jit(solution)/shard_map/jit(_cho_solve)/triangular_solve | solution.py:85
  302.2 95.9 %all-reduce.1 = (f32[]{:T(128)}, f32[]{:T(128)}) all-reduce(f32[]{:T(128)} %get-tuple-element.72, f32[]{:T(128)} %get-tuple-element.71), channel_id=1, replica_groups=mesh['gx'=32,'gy'=16] {'gx','gy'}, use_global_device_ids=true, to_apply=%region_1.2 | all-reduce | flops 2 | bytes 16 | tf_op jit(solution)/shard_map/psum | solution.py:23
  429.0 23.0 %psum.95 = f32[512]{0:T(512)S(1)} all-reduce(f32[512]{0:T(512)S(1)} %bitcast.1268), channel_id=1, replica_groups=mesh['gx'=32,'gy'=16] {'gy'}, use_global_device_ids=true, to_apply=%region_14.16 | all-reduce | flops 512 | bytes 4096 | tf_op jit(solution)/shard_map/psum | solution.py:82
  481.4 95.9 %psum.96 = f32[]{:T(128)} all-reduce(f32[]{:T(128)} %get-tuple-element.93), channel_id=1, replica_groups=mesh['gx'=32,'gy'=16] {'gx','gy'}, use_global_device_ids=true, to_apply=%region_16.18 | all-reduce | flops 1 | bytes 8 | tf_op jit(solution)/shard_map/psum | solution.py:23
  598.6 9.4 fusion.446
  608.3 23.0 %psum.97 = f32[512]{0:T(512)S(1)} all-reduce(f32[512]{0:T(512)S(1)} %bitcast.1269), channel_id=1, replica_groups=mesh['gx'=32,'gy'=16] {'gy'}, use_global_device_ids=true, to_apply=%region_17.19 | all-reduce | flops 512 | bytes 4096 | tf_op jit(solution)/shard_map/psum | solution.py:82
  660.7 95.9 %psum.98 = f32[]{:T(128)} all-reduce(f32[]{:T(128)} %fusion.229), channel_id=1, replica_groups=mesh['gx'=32,'gy'=16] {'gx','gy'}, use_global_device_ids=true, to_apply=%region_19.21 | all-reduce | flops 1 | bytes 8 | tf_op jit(solution)/shard_map/psum | solution.py:105
  777.8 9.4 fusion.449
  787.5 23.0 %psum.99 = f32[512]{0:T(512)S(1)} all-reduce(f32[512]{0:T(512)S(1)} %bitcast.1270), channel_id=1, replica_groups=mesh['gx'=32,'gy'=16] {'gy'}, use_global_device_ids=true, to_apply=%region_20.22 | all-reduce | flops 512 | bytes 4096 | tf_op jit(solution)/shard_map/psum | solution.py:82
  839.9 96.1 %psum.100 = f32[]{:T(128)} all-reduce(f32[]{:T(128)} %get-tuple-element.87), channel_id=1, replica_groups=mesh['gx'=32,'gy'=16] {'gx','gy'}, use_global_device_ids=true, to_apply=%region_22.24 | all-reduce | flops 1 | bytes 8 | tf_op jit(solution)/shard_map/psum | solution.py:23
  966.9 23.0 %psum.101 = f32[512]{0:T(512)S(1)} all-reduce(f32[512]{0:T(512)S(1)} %bitcast.1271), channel_id=1, replica_groups=mesh['gx'=32,'gy'=16] {'gy'}, use_global_device_ids=true, to_apply=%region_23.25 | all-reduce | flops 512 | bytes 4096 | tf_op jit(solution)/shard_map/psum | solution.py:82
  1019.2 95.9 %psum.102 = f32[]{:T(128)} all-reduce(f32[]{:T(128)} %fusion.216), channel_id=1, replica_groups=mesh['gx'=32,'gy'=16] {'gx','gy'}, use_global_device_ids=true, to_apply=%region_25.27 | all-reduce | flops 1 | bytes 8 | tf_op jit(solution)/shard_map/psum | solution.py:105
  1146.0 23.0 %psum.103 = f32[512]{0:T(512)S(1)} all-reduce(f32[512]{0:T(512)S(1)} %bitcast.1272), channel_id=1, replica_groups=mesh['gx'=32,'gy'=16] {'gy'}, use_global_device_ids=true, to_apply=%region_26.28 | all-reduce | flops 512 | bytes 4096 | tf_op jit(solution)/shard_map/psum | solution.py:82
  (362 shorter events, 352.6 us)
Async XLA Ops:
  7.2 131.7 %all-reduce.4.cloned.1.call-start = ((), (), s32[]{:S(2)}) async-start(), calls=%async_computation | async-start | bytes 2097152 | tf_op jit(solution)/shard_map/psum | solution.py:65
  8.0 20.4 %collective-permute-start.1 = (f32[1,1,8,128]{3,2,1,0:T(8,128)S(1)}, f32[1,1,8,128]{3,2,1,0:T(8,128)S(1)}, u32[]{:S(2)}, u32[]{:S(2)}) collective-permute-start(f32[1,1,8,128]{3,2,1,0:T(8,128)S(1)} %get-tuple-element.98), channel_id=1, source_target_pairs={{0,16},{16,32},{32,48},{48,64},{64,80},{80,96},{96,112},{112,128},... | collective-permute-start | bytes 12296 | tf_op jit(solution)/shard_map/ppermute | solution.py:14
  11.1 17.3 %collective-permute-start = (f32[1,1,8,128]{3,2,1,0:T(8,128)S(1)}, f32[1,1,8,128]{3,2,1,0:T(8,128)S(1)}, u32[]{:S(2)}, u32[]{:S(2)}) collective-permute-start(f32[1,1,8,128]{3,2,1,0:T(8,128)S(1)} %get-tuple-element.98), channel_id=1, source_target_pairs={{16,0},{32,16},{48,32},{64,48},{80,64},{96,80},{112,96},{128,112},... | collective-permute-start | bytes 12296 | tf_op jit(solution)/shard_map/ppermute | solution.py:17
  28.4 12.6 %collective-permute-start.3 = (f32[3,1,8,128]{3,2,1,0:T(8,128)S(1)}, f32[3,1,8,128]{3,2,1,0:T(8,128)S(1)}, u32[]{:S(2)}, u32[]{:S(2)}) collective-permute-start(f32[3,1,8,128]{3,2,1,0:T(8,128)S(1)} %pad_maximum_fusion.6), channel_id=1, source_target_pairs={{0,1},{1,2},{2,3},{3,4},{4,5},{5,6},{6,7},{7,8},{8,9},{9,10},{10,1... | collective-permute-start | bytes 36872 | tf_op jit(solution)/shard_map/ppermute | solution.py:14
  399.5 8.6 collective-permute-start.9
  408.8 9.9 collective-permute-start.11
  455.8 9.2 collective-permute-start.13
  471.2 8.4 collective-permute-start.15
  578.6 8.6 collective-permute-start.17
  588.0 10.1 collective-permute-start.19
  635.2 9.2 collective-permute-start.21
  650.6 8.4 collective-permute-start.23
  758.0 8.6 collective-permute-start.25
  767.3 9.9 collective-permute-start.27
  814.3 9.2 collective-permute-start.29
  829.7 8.4 collective-permute-start.31
  937.3 8.6 collective-permute-start.33
  946.7 9.9 collective-permute-start.35
  993.7 9.2 collective-permute-start.37
  1009.1 8.4 collective-permute-start.39
  1116.5 8.6 collective-permute-start.41
  1125.8 9.9 collective-permute-start.43
  1172.8 9.2 collective-permute-start.45
  1188.2 8.4 collective-permute-start.47
  (32 other events, 828.6 us)
Sparse Core Ops, SparseCore 0:
  21.6 117.2 all-reduce.3
where the time goes:
time: 1210 us
  blocking collectives  618 us (51%)
  starting transfers between devices  189 us (16%)
  waiting for transfers between devices  138 us (11%)
  other arithmetic  128 us (11%)
  matrix products  95.8 us (8%)
  between operations  25.5 us (2%)
    psum x3, blocking collectives, weighted_norm(): return lax.psum(jnp.sum(residual * precond), ('gx', 'gy'))  288 us
    psum x2, blocking collectives, shards(): alpha = norm_now / lax.psum(jnp.sum(direction * image), ('gx', 'gy'))  192 us
    psum x6, blocking collectives, operate(): lax.psum(jnp.einsum('sco,sc->o', own_hot, corner_values, precision=highes...  138 us
    ppermute x24, starting transfers between devices, extended(): lax.ppermute(lax.slice_in_dim(block, 0, width, axis=dim), axis, backward)  96.5 us
    ppermute x24, starting transfers between devices, extended(): lax.ppermute(lax.slice_in_dim(block, block.shape[dim] - width, None, axis...  92.8 us
    another operation x14, other arithmetic, shards(): lower = jnp.linalg.cholesky(system)  78.8 us
    psum x1, waiting for transfers between devices, shards(): lax.psum(jnp.einsum('sod,sdp->op', spread, own_hot, precision=highest), '...  64.5 us
    dot_general x6, matrix products, operate(): result = jnp.einsum('sij,sj->si', schur, gathered, precision=highest)  56.7 us
  transfers between devices with their start and end apart: 49, of which 24 were waited for; matrix products, arithmetic and copies ran while one was open for 2% of the time, Pallas kernels for 0%

commit v1 on v0

--- a/solution.py
+++ b/solution.py
@@ -62,7 +62,9 @@
     coarse_iota = lax.iota(jnp.int32, coarse_size)
     own_hot = (corner_map[0, 0][:, :, None] == coarse_iota[None, None, :]).astype(jnp.float32)
     spread = jnp.einsum("sco,scd->sod", own_hot, corner_block, precision=highest)
-    assembled = lax.psum(jnp.einsum("sod,sdp->op", spread, own_hot, precision=highest), "gy")
+    assembled = jnp.sum(
+        lax.all_gather(jnp.einsum("sod,sdp->op", spread, own_hot, precision=highest), "gy"), axis=0
+    )
     coarse_eye = (coarse_iota[:, None] == coarse_iota[None, :]).astype(jnp.float32)
     system = assembled + coarse_diag[0][:, None] * coarse_eye
     lower = jnp.linalg.cholesky(system)

time: 1210 us -> 1190 us (0.983)
  the two profiles are of different devices: /device:TPU:225 before, /device:TPU:223 now
where the time goes in v1:
time: 1190 us; the launch traced here: 1180 us
  blocking collectives  608 us (51%)
  starting transfers between devices  198 us (17%)
  other arithmetic  133 us (11%)
  waiting for transfers between devices  110 us (9%)
  matrix products  99.6 us (8%)
  between operations  25.5 us (2%)
    psum x3, blocking collectives, weighted_norm(): return lax.psum(jnp.sum(residual * precond), ('gx', 'gy'))  278 us
    psum x2, blocking collectives, shards(): alpha = norm_now / lax.psum(jnp.sum(direction * image), ('gx', 'gy'))  186 us
    psum x6, blocking collectives, operate(): lax.psum(jnp.einsum('sco,sc->o', own_hot, corner_values, precision=highes...  144 us
    ppermute x24, starting transfers between devices, extended(): lax.ppermute(lax.slice_in_dim(block, block.shape[dim] - width, None, axis...  137 us
    another operation x14, other arithmetic, shards(): lower = jnp.linalg.cholesky(system)  79.1 us
    ppermute x24, waiting for transfers between devices, extended(): lax.ppermute(lax.slice_in_dim(block, 0, width, axis=dim), axis, backward)  63.3 us
    ppermute x24, starting transfers between devices, extended(): lax.ppermute(lax.slice_in_dim(block, 0, width, axis=dim), axis, backward)  60.9 us
    dot_general x6, matrix products, operate(): result = jnp.einsum('sij,sj->si', schur, gathered, precision=highest)  57.1 us
  transfers between devices with their start and end apart: 49, of which 24 were waited for; matrix products, arithmetic and copies ran while one was open for 2% of the time, Pallas kernels for 0%

profile of v1, /device:TPU:223, one launch (start us, length us, event | category | flops | bytes accessed | tf_op | source)
XLA Modules:
  0.0 1184.0 jit_solution(7218659849683364241)
XLA Ops:
  38.5 25.8 %psum.85 = f32[512]{0:T(512)S(1)} all-reduce(f32[512]{0:T(512)S(1)} %bitcast.1268), channel_id=1, replica_groups=mesh['gx'=32,'gy'=16] {'gy'}, use_global_device_ids=true, to_apply=%region_11.12 | all-reduce | flops 512 | bytes 4096 | tf_op jit(solution)/shard_map/psum | solution.py:84
  64.3 9.7 fusion.439
  74.0 38.9 %all-gather.3.cloned.1.call-done = f32[8192,512]{1,0:T(8,128)} async-done(((f32[512,512]{1,0:T(8,128)}), f32[8192,512]{1,0:T(8,128)}) %all-gather.3.cloned.1.call-update) | async-done | bytes 16777232 | tf_op jit(solution)/shard_map/all_gather | solution.py:66
  122.5 11.7 cholesky.103
  134.3 9.8 custom-call.32
  146.7 12.2 %cholesky.215 = f32[128,128]{1,0:T(8,128)S(1)} custom-call(f32[128,128]{1,0:T(8,128)S(1)} %cholesky.267), custom_call_target="Cholesky" | custom-call | tf_op jit(solution)/shard_map/jit(cholesky)/cholesky | solution.py:70
  158.9 9.8 custom-call.33
  170.3 11.7 cholesky.236
  182.8 9.8 custom-call.34
  194.0 11.9 %cholesky.253 = f32[128,128]{1,0:T(8,128)S(1)} custom-call(f32[128,128]{1,0:T(8,128)S(1)} %convolution_subtract_fusion.2), custom_call_target="Cholesky" | custom-call | tf_op jit(solution)/shard_map/jit(cholesky)/cholesky | solution.py:70
  218.5 39.3 %custom-call.40 = f32[4,128,128]{1,2,0:T(8,128)S(1)} custom-call(f32[4,128,128]{2,1,0:T(8,128)S(1)} %get-tuple-element.41), custom_call_target="InvertDiagBlocksLowerTriangular" | custom-call | tf_op jit(solution)/shard_map/jit(_cho_solve)/triangular_solve | solution.py:87
  285.0 92.8 %all-reduce.1 = (f32[]{:T(128)}, f32[]{:T(128)}) all-reduce(f32[]{:T(128)} %get-tuple-element.48, f32[]{:T(128)} %get-tuple-element.47), channel_id=1, replica_groups=mesh['gx'=32,'gy'=16] {'gx','gy'}, use_global_device_ids=true, to_apply=%region_1.2 | all-reduce | flops 2 | bytes 16 | tf_op jit(solution)/shard_map/psum | solution.py:23
  396.8 9.4 fusion.442
  406.8 23.8 %psum.87 = f32[512]{0:T(512)S(1)} all-reduce(f32[512]{0:T(512)S(1)} %bitcast.1269), channel_id=1, replica_groups=mesh['gx'=32,'gy'=16] {'gy'}, use_global_device_ids=true, to_apply=%region_14.16 | all-reduce | flops 512 | bytes 4096 | tf_op jit(solution)/shard_map/psum | solution.py:84
  463.5 92.8 %psum.88 = f32[]{:T(128)} all-reduce(f32[]{:T(128)} %get-tuple-element.69), channel_id=1, replica_groups=mesh['gx'=32,'gy'=16] {'gx','gy'}, use_global_device_ids=true, to_apply=%region_16.18 | all-reduce | flops 1 | bytes 8 | tf_op jit(solution)/shard_map/psum | solution.py:23
  585.2 23.6 %psum.89 = f32[512]{0:T(512)S(1)} all-reduce(f32[512]{0:T(512)S(1)} %bitcast.1270), channel_id=1, replica_groups=mesh['gx'=32,'gy'=16] {'gy'}, use_global_device_ids=true, to_apply=%region_17.19 | all-reduce | flops 512 | bytes 4096 | tf_op jit(solution)/shard_map/psum | solution.py:84
  641.7 92.8 %psum.90 = f32[]{:T(128)} all-reduce(f32[]{:T(128)} %fusion.228), channel_id=1, replica_groups=mesh['gx'=32,'gy'=16] {'gx','gy'}, use_global_device_ids=true, to_apply=%region_19.21 | all-reduce | flops 1 | bytes 8 | tf_op jit(solution)/shard_map/psum | solution.py:107
  753.5 9.8 fusion.448
  763.9 23.6 %psum.91 = f32[512]{0:T(512)S(1)} all-reduce(f32[512]{0:T(512)S(1)} %bitcast.1271), channel_id=1, replica_groups=mesh['gx'=32,'gy'=16] {'gy'}, use_global_device_ids=true, to_apply=%region_20.22 | all-reduce | flops 512 | bytes 4096 | tf_op jit(solution)/shard_map/psum | solution.py:84
  820.3 92.8 %psum.92 = f32[]{:T(128)} all-reduce(f32[]{:T(128)} %get-tuple-element.63), channel_id=1, replica_groups=mesh['gx'=32,'gy'=16] {'gx','gy'}, use_global_device_ids=true, to_apply=%region_22.24 | all-reduce | flops 1 | bytes 8 | tf_op jit(solution)/shard_map/psum | solution.py:23
  932.1 9.4 fusion.451
  942.1 23.6 %psum.93 = f32[512]{0:T(512)S(1)} all-reduce(f32[512]{0:T(512)S(1)} %bitcast.1272), channel_id=1, replica_groups=mesh['gx'=32,'gy'=16] {'gy'}, use_global_device_ids=true, to_apply=%region_23.25 | all-reduce | flops 512 | bytes 4096 | tf_op jit(solution)/shard_map/psum | solution.py:84
  998.6 93.0 %psum.94 = f32[]{:T(128)} all-reduce(f32[]{:T(128)} %fusion.215), channel_id=1, replica_groups=mesh['gx'=32,'gy'=16] {'gx','gy'}, use_global_device_ids=true, to_apply=%region_25.27 | all-reduce | flops 1 | bytes 8 | tf_op jit(solution)/shard_map/psum | solution.py:107
  1120.5 23.6 %psum.95 = f32[512]{0:T(512)S(1)} all-reduce(f32[512]{0:T(512)S(1)} %bitcast.1273), channel_id=1, replica_groups=mesh['gx'=32,'gy'=16] {'gy'}, use_global_device_ids=true, to_apply=%region_26.28 | all-reduce | flops 512 | bytes 4096 | tf_op jit(solution)/shard_map/psum | solution.py:84
  (347 shorter events, 365.5 us)
Async XLA Ops:
  7.2 105.7 %all-gather.3.cloned.1.call-start = ((), (), s32[]{:S(2)}) async-start(), calls=%async_computation | async-start | bytes 17825792 | tf_op jit(solution)/shard_map/all_gather | solution.py:66
  12.9 15.5 %collective-permute-start = (f32[1,1,8,128]{3,2,1,0:T(8,128)S(1)}, f32[1,1,8,128]{3,2,1,0:T(8,128)S(1)}, u32[]{:S(2)}, u32[]{:S(2)}) collective-permute-start(f32[1,1,8,128]{3,2,1,0:T(8,128)S(1)} %get-tuple-element.74), channel_id=1, source_target_pairs={{16,0},{32,16},{48,32},{64,48},{80,64},{96,80},{112,96},{128,112},... | collective-permute-start | bytes 12296 | tf_op jit(solution)/shard_map/ppermute | solution.py:17
  15.4 13.1 %collective-permute-start.1 = (f32[1,1,8,128]{3,2,1,0:T(8,128)S(1)}, f32[1,1,8,128]{3,2,1,0:T(8,128)S(1)}, u32[]{:S(2)}, u32[]{:S(2)}) collective-permute-start(f32[1,1,8,128]{3,2,1,0:T(8,128)S(1)} %get-tuple-element.74), channel_id=1, source_target_pairs={{0,16},{16,32},{32,48},{48,64},{64,80},{80,96},{96,112},{112,128},... | collective-permute-start | bytes 12296 | tf_op jit(solution)/shard_map/ppermute | solution.py:14
  28.5 8.5 collective-permute-start.2
  266.0 7.8 collective-permute-start.5
  379.2 8.6 collective-permute-start.8
  434.4 9.2 collective-permute-start.12
  441.6 7.8 collective-permute-start.13
  449.4 8.8 collective-permute-start.14
  557.6 8.6 collective-permute-start.16
  612.6 9.2 collective-permute-start.20
  619.9 7.8 collective-permute-start.21
  627.7 8.8 collective-permute-start.22
  735.9 8.6 collective-permute-start.24
  791.3 9.2 collective-permute-start.28
  798.5 7.8 collective-permute-start.29
  806.3 8.8 collective-permute-start.30
  914.5 8.6 collective-permute-start.32
  969.5 9.2 collective-permute-start.36
  976.7 7.8 collective-permute-start.37
  984.5 8.8 collective-permute-start.38
  1092.9 8.6 collective-permute-start.40
  1147.9 9.2 collective-permute-start.44
  1163.0 8.8 collective-permute-start.46
  (33 other events, 750.2 us)
Sparse Core Ops, SparseCore 0:
  12.3 100.5 all-gather.2
